TPU v7x, 32 devices: a whole 2x2x4 slice. The times are simulated.
32 devices in a mesh: tm: 8 (over z, y), head: 4 (over x, core).
Axes of the slice: x: 2, y: 2, z: 4, core: 2. Of those that a mesh axis runs over, the one named last changes fastest.
Arguments:
- tokens: bfloat16 [2048, 1024], P('tm'), may hold values from -24 to 24
- q_weight: bfloat16 [1024, 1024], P(None, 'head'), may hold values from -2 to 2
- k_weight: bfloat16 [1024, 1024], P(None, 'head'), may hold values from -2 to 2
- v_weight: bfloat16 [1024, 1024], P(None, 'head'), may hold values from -0.1875 to 0.1875
- o_weight: bfloat16 [1024, 1024], P('head'), may hold values from -0.1875 to 0.1875
- rand_blocks: int32 [16, 3], P('tm'), may hold values from 0 to 15, as said below
- global_pos: int32 [256], replicated, may hold values from 0 to 2047, as said below
Outputs:
- mixed_out: bfloat16 [2048, 1024], P(('tm', 'head'))
Inputs may be any that keep to these rules, and one draw needn't show every extreme that they name: rand_blocks[b, r] names a block whose shard index (block // 2) differs from that of b by at most 2; in every draw some entry differs by exactly 2. `global_pos`: 256 distinct positions in ascending order.
All inputs are finite; a program needn't handle non-finite values.
Results may differ from a plain program's by a relative error of at most 0.011.
Values may be sent and summed in bfloat16 or wider, within the bound.
No kernel may reach another device: no remote copies, remote signals or barrier semaphores. Data moves between devices by JAX's collectives and lax.ppermute only.
A program may use at most 64 MiB of HBM per device.

v0:
```python
import jax
import jax.numpy as jnp
from jax import lax
from jax.sharding import PartitionSpec as P

HEAD_DIM = 64
BLOCK = 128
GLOBALS = 256
RAND = 3
SPREAD = 2


def shifted(block, axis, distance):
    devices = range(lax.axis_size(axis))
    route = [(i - distance, i) for i in devices if i - distance in devices]
    return lax.ppermute(block, axis, route)


def shards(tokens, q_weight, k_weight, v_weight, o_weight, rand_blocks, global_pos):
    tok_rows = tokens.shape[0]
    feats = q_weight.shape[1]
    heads_here = feats // HEAD_DIM
    per_shard = tok_rows // BLOCK
    shard_count = lax.axis_size("tm")
    shard_index = lax.axis_index("tm")
    score_scale = HEAD_DIM ** (-0.5)
    queries = jnp.dot(tokens, q_weight, preferred_element_type=jnp.float32).astype(jnp.bfloat16)
    keys_here = jnp.dot(tokens, k_weight, preferred_element_type=jnp.float32).astype(jnp.bfloat16)
    values_here = jnp.dot(tokens, v_weight, preferred_element_type=jnp.float32).astype(jnp.bfloat16)
    key_value = jnp.concatenate([keys_here, values_here], axis=1)
    positions = shard_index * tok_rows + jnp.arange(tok_rows, dtype=jnp.int32)
    picked = global_pos[:, None] == positions[None, :]
    pick_table = picked.astype(jnp.bfloat16)
    projected = jnp.concatenate([queries, key_value], axis=1)
    summed_rows = lax.psum(
        jnp.dot(pick_table, projected, preferred_element_type=jnp.float32), "tm"
    ).astype(jnp.bfloat16)
    global_q = summed_rows[:, :feats]
    global_k = summed_rows[:, feats : 2 * feats]
    global_v = summed_rows[:, 2 * feats :]
    offsets = list(range(SPREAD, 0, -1)) + list(range(-1, -SPREAD - 1, -1))
    fetched = [shifted(key_value, "tm", offset) for offset in offsets]
    earlier = fetched[:SPREAD]
    later_keys = fetched[SPREAD:]
    extended = jnp.concatenate(earlier + [key_value] + later_keys, axis=0).reshape(
        -1, BLOCK, 2 * feats
    )
    own_first = SPREAD * per_shard
    window = jnp.stack(
        [
            extended[own_first + shift_by : own_first + shift_by + per_shard]
            for shift_by in (-2, -1, 0, 1)
        ],
        axis=1,
    )
    chosen = extended[rand_blocks - (shard_index - SPREAD) * per_shard]
    gathered_keys = jnp.concatenate([window, chosen], axis=1).reshape(per_shard, -1, 2 * feats)
    key_length = gathered_keys.shape[1]
    block_ids = (
        shard_index * per_shard
        + jnp.arange(per_shard, dtype=jnp.int32)[:, None]
        + jnp.arange(-2, 2, dtype=jnp.int32)[None, :]
    )
    inside = (block_ids >= 0) & (block_ids < shard_count * per_shard)
    valid_keys = jnp.concatenate(
        [jnp.repeat(inside, BLOCK, axis=1), jnp.ones((per_shard, RAND * BLOCK), dtype=bool)], axis=1
    )
    block_q = queries.reshape(per_shard, BLOCK, heads_here, HEAD_DIM)
    near_k = gathered_keys[:, :, :feats].reshape(per_shard, key_length, heads_here, HEAD_DIM)
    near_v = gathered_keys[:, :, feats:].reshape(per_shard, key_length, heads_here, HEAD_DIM)
    glob_k4 = global_k.reshape(GLOBALS, heads_here, HEAD_DIM)
    glob_v4 = global_v.reshape(GLOBALS, heads_here, HEAD_DIM)
    near_scores = (
        jnp.einsum("jqhd,jkhd->jhqk", block_q, near_k, preferred_element_type=jnp.float32)
        * score_scale
    )
    near_scores = jnp.where(valid_keys[:, None, None, :], near_scores, -jnp.inf)
    far_scores = (
        jnp.einsum("jqhd,ghd->jhqg", block_q, glob_k4, preferred_element_type=jnp.float32)
        * score_scale
    )
    row_max = jnp.maximum(jnp.max(near_scores, axis=3), jnp.max(far_scores, axis=3))
    near_exp = jnp.exp(near_scores - row_max[..., None])
    far_exp = jnp.exp(far_scores - row_max[..., None])
    denominator = jnp.sum(near_exp, axis=3) + jnp.sum(far_exp, axis=3)
    numerator = jnp.einsum(
        "jhqk,jkhd->jqhd", near_exp.astype(jnp.bfloat16), near_v, preferred_element_type=jnp.float32
    )
    numerator = numerator + jnp.einsum(
        "jhqg,ghd->jqhd", far_exp.astype(jnp.bfloat16), glob_v4, preferred_element_type=jnp.float32
    )
    local_out = (
        (numerator / jnp.transpose(denominator, (0, 2, 1))[..., None])
        .astype(jnp.bfloat16)
        .reshape(tok_rows, feats)
    )
    glob_q4 = global_q.reshape(GLOBALS, heads_here, HEAD_DIM)
    local_k4 = keys_here.reshape(tok_rows, heads_here, HEAD_DIM)
    glob_scores = (
        jnp.einsum("ghd,thd->hgt", glob_q4, local_k4, preferred_element_type=jnp.float32)
        * score_scale
    )
    local_max = jnp.max(glob_scores, axis=2)
    glob_exp = jnp.exp(glob_scores - local_max[..., None])
    local_totals = jnp.sum(glob_exp, axis=2)
    local_values = values_here.astype(jnp.float32).reshape(tok_rows, heads_here, HEAD_DIM)
    local_accum = jnp.einsum(
        "hgt,thd->hgd", glob_exp, local_values, precision=lax.Precision.HIGHEST
    )
    peak = lax.pmax(local_max, "tm")
    rescale = jnp.exp(local_max - peak)
    totals, accumulated = lax.psum((local_totals * rescale, local_accum * rescale[..., None]), "tm")
    global_out = (accumulated / totals[..., None]).astype(jnp.bfloat16)
    global_out = jnp.transpose(global_out, (1, 0, 2)).reshape(GLOBALS, feats)
    placed = jnp.einsum(
        "gt,gf->tf", pick_table, global_out, preferred_element_type=jnp.float32
    ).astype(jnp.bfloat16)
    is_global = jnp.any(picked, axis=0)
    attended = jnp.where(is_global[:, None], placed, local_out)
    mixed_out = lax.psum_scatter(
        jnp.dot(attended, o_weight, preferred_element_type=jnp.float32),
        "head",
        scatter_dimension=0,
        tiled=True,
    )
    return mixed_out.astype(jnp.bfloat16)


def solution(mesh):
    placed = (
        P("tm", None),
        P(None, "head"),
        P(None, "head"),
        P(None, "head"),
        P("head", None),
        P("tm", None),
        P(),
    )
    return jax.shard_map(
        shards, mesh=mesh, in_specs=placed, out_specs=P(("tm", "head"), None), check_vma=False
    )
```

profile of v0, /device:TPU:0, one launch (start us, length us, event | category | flops | bytes accessed | tf_op | source)
XLA Modules:
  0.0 196.0 jit_solution(11673844784302354247)
XLA Ops:
  6.6 1.7 convolution_convert_fusion
  8.2 1.5 convolution_convert_fusion.1
  9.8 4.9 %collective-permute-start = (bf16[256,512]{0,1:T(8,128)(2,1)S(1)}, bf16[256,512]{0,1:T(8,128)(2,1)S(1)}, u32[]{:S(2)}, u32[]{:S(2)}) collective-permute-start(bf16[256,512]{0,1:T(8,128)(2,1)S(1)} %pad_maximum_fusion.4), channel_id=1, source_target_pairs={{0,4},{4,8},{8,12},{12,16},{16,20},{20,24},{24,28},{1,5},{5,9},{9,... | collective-permute-start | bytes 786440 | tf_op jit(solution)/shard_map/ppermute | solution.py:16
  14.7 4.2 %collective-permute-start.2 = (bf16[256,512]{0,1:T(8,128)(2,1)S(1)}, bf16[256,512]{0,1:T(8,128)(2,1)}, u32[]{:S(2)}, u32[]{:S(2)}) collective-permute-start(bf16[256,512]{0,1:T(8,128)(2,1)S(1)} %pad_maximum_fusion.4), channel_id=1, source_target_pairs={{0,8},{4,12},{8,16},{12,20},{16,24},{20,28},{1,9},{5,13},{9,17},{1... | collective-permute-start | bytes 786440 | tf_op jit(solution)/shard_map/ppermute | solution.py:16
  18.9 1.3 collective-permute-start.1
  20.2 1.3 collective-permute-start.3
  22.4 49.3 %all-reduce.5 = bf16[256,768]{1,0:T(8,128)(2,1)S(1)} all-reduce(f32[256,768]{1,0:T(8,128)S(1)} %fusion.20), channel_id=1, replica_groups=mesh['tm'=8,'head'=4] {'tm'}, use_global_device_ids=true, to_apply=%region_1.2 | all-reduce | flops 196608 | bytes 1179648 | tf_op jit(solution)/shard_map/psum | solution.py:35
  72.3 20.2 %pmax.7 = f32[4,256]{1,0:T(4,128)S(1)} all-reduce(f32[4,256]{1,0:T(4,128)S(1)} %get-tuple-element.21), channel_id=1, replica_groups=mesh['tm'=8,'head'=4] {'tm'}, use_global_device_ids=true, to_apply=%region_3.4 | all-reduce | flops 1024 | bytes 8192 | tf_op jit(solution)/shard_map/pmax | solution.py:110
  92.6 1.3 convolution_multiply_fusion.2
  95.8 17.1 %psum.23 = f32[4,256]{1,0:T(4,128)S(1)} all-reduce(f32[4,256]{1,0:T(4,128)S(1)} %get-tuple-element.5), channel_id=1, replica_groups=mesh['tm'=8,'head'=4] {'tm'}, use_global_device_ids=true, to_apply=%region_6.7 | all-reduce | flops 1024 | bytes 8192 | tf_op jit(solution)/shard_map/psum | solution.py:112
  113.6 1.7 constant_dynamic-update-slice_fusion.4
  116.8 1.8 constant_dynamic-update-slice_fusion.1
  120.5 1.7 constant_dynamic-update-slice_fusion
  122.2 1.6 copy.78
  123.8 1.7 constant_dynamic-update-slice_fusion.8
  126.9 1.5 gather_fusion
  128.4 2.1 %constant_dynamic-update-slice_fusion.5 = bf16[2,7,128,512]{3,2,1,0:T(8,128)(2,1)} fusion(bf16[2,7,128,512]{3,2,1,0:T(8,128)(2,1)} %constant_dynamic-update-slice_fusion.6, bf16[2,3,128,512]{3,2,1,0:T(8,128)(2,1)} %bitcast.63), kind=kLoop, calls=%fused_computation.58 | loop fusion | bytes 1572864 | tf_op jit(solution)/shard_map/concatenate | solution.py:57
  130.5 2.5 %fusion.42 = (bf16[2,896,256]{2,1,0:T(8,128)(2,1)}, bf16[2,896,256]{2,1,0:T(8,128)(2,1)S(1)}) fusion(bf16[2,896,512]{2,1,0:T(8,128)(2,1)} %bitcast.64), kind=kLoop, calls=%fused_computation.79 | loop fusion | bytes 3670016 | tf_op jit(solution)/shard_map/slice | solution.py:69
  133.0 1.5 copy.84
  137.8 3.1 %fusion.9 = f32[2,128,4,64]{1,3,2,0:T(8,128)S(1)} fusion(bf16[2,896,4,64]{1,3,2,0:T(8,128)(2,1)S(1)} %bitcast.69, f32[2,4,128,896]{3,2,1,0:T(8,128)} %copy-done.1, f32[2,4,128]{2,1,0:T(4,128)S(1)} %copy_maximum_fusion, pred[2,896]{1,0:T(4,128)(4,1)S(1)} %concatenate.28), kind=kOutput, calls=%fused_computation.14 | convolution fusion | flops 121110528 | bytes 4855552 | tf_op jit(solution)/shard_map/jhqk,jkhd->jqhd/dot_general | solution.py:86
  141.8 18.8 %all-reduce.4.cloned.1.call-done = f32[4,256,64]{1,2,0:T(8,128)} async-done(((f32[4,256,64]{1,2,0:T(8,128)}), f32[4,256,64]{1,2,0:T(8,128)}) %all-reduce.4.cloned.1.call-update) | async-done | bytes 262160 | tf_op jit(solution)/shard_map/psum | solution.py:112
  161.6 1.6 fusion.14
  163.2 24.3 %reduce-scatter.2.cloned.1.call-done = f32[64,1024]{1,0:T(8,128)} async-done(((f32[256,1024]{1,0:T(8,128)}), f32[64,1024]{1,0:T(8,128)}) %reduce-scatter.2.cloned.1.call-update) | async-done | bytes 262160 | tf_op jit(solution)/shard_map/reduce_scatter | solution.py:120
  187.5 1.6 convert_element_type.41
  (77 shorter events, 13.8 us)
Async XLA Ops:
  6.5 155.0 %copy-start = (bf16[256,1024]{1,0:T(8,128)(2,1)S(1)}, bf16[256,1024]{1,0:T(8,128)(2,1)}, u32[]{:S(2)}) copy-start(bf16[256,1024]{1,0:T(8,128)(2,1)} %param.11) | copy-start | bytes 1572868
  6.5 14.9 %copy-start.2 = (bf16[256,1024]{1,0:T(8,128)(2,1)S(1)}, bf16[256,1024]{1,0:T(8,128)(2,1)}, u32[]{:S(2)}) copy-start(bf16[256,1024]{1,0:T(8,128)(2,1)} %param.7) | copy-start | bytes 1572868
  6.5 15.0 %copy-start.3 = (bf16[1024,256]{1,0:T(8,128)(2,1)S(1)}, bf16[1024,256]{1,0:T(8,128)(2,1)}, u32[]{:S(2)}) copy-start(bf16[1024,256]{1,0:T(8,128)(2,1)} %param.8) | copy-start | bytes 1572868
  6.5 15.5 %copy-start.5 = (s32[256]{0:T(256)S(1)}, s32[256]{0:T(256)}, u32[]{:S(2)}) copy-start(s32[256]{0:T(256)} %param.13) | copy-start | bytes 3076
  6.5 154.0 %all-reduce.4.cloned.1.call-start = ((), (), s32[]{:S(2)}) async-start(), calls=%async_computation.1 | async-start | bytes 524288 | tf_op jit(solution)/shard_map/psum | solution.py:112
  9.8 105.4 %collective-permute-start = (bf16[256,512]{0,1:T(8,128)(2,1)S(1)}, bf16[256,512]{0,1:T(8,128)(2,1)S(1)}, u32[]{:S(2)}, u32[]{:S(2)}) collective-permute-start(bf16[256,512]{0,1:T(8,128)(2,1)S(1)} %pad_maximum_fusion.4), channel_id=1, source_target_pairs={{0,4},{4,8},{8,12},{12,16},{16,20},{20,24},{24,28},{1,5},{5,9},{9,... | collective-permute-start | bytes 786440 | tf_op jit(solution)/shard_map/ppermute | solution.py:16
  14.7 98.9 %collective-permute-start.2 = (bf16[256,512]{0,1:T(8,128)(2,1)S(1)}, bf16[256,512]{0,1:T(8,128)(2,1)}, u32[]{:S(2)}, u32[]{:S(2)}) collective-permute-start(bf16[256,512]{0,1:T(8,128)(2,1)S(1)} %pad_maximum_fusion.4), channel_id=1, source_target_pairs={{0,8},{4,12},{8,16},{12,20},{16,24},{20,28},{1,9},{5,13},{9,17},{1... | collective-permute-start | bytes 786440 | tf_op jit(solution)/shard_map/ppermute | solution.py:16
  18.9 97.9 %collective-permute-start.1 = (bf16[256,512]{0,1:T(8,128)(2,1)S(1)}, bf16[256,512]{0,1:T(8,128)(2,1)}, u32[]{:S(2)}, u32[]{:S(2)}) collective-permute-start(bf16[256,512]{0,1:T(8,128)(2,1)S(1)} %pad_maximum_fusion.4), channel_id=1, source_target_pairs={{4,0},{8,4},{12,8},{16,12},{20,16},{24,20},{28,24},{5,1},{9,5},{13... | collective-permute-start | bytes 786440 | tf_op jit(solution)/shard_map/ppermute | solution.py:16
  20.2 100.3 %collective-permute-start.3 = (bf16[256,512]{0,1:T(8,128)(2,1)S(1)}, bf16[256,512]{0,1:T(8,128)(2,1)}, u32[]{:S(2)}, u32[]{:S(2)}) collective-permute-start(bf16[256,512]{0,1:T(8,128)(2,1)S(1)} %pad_maximum_fusion.4), channel_id=1, source_target_pairs={{8,0},{12,4},{16,8},{20,12},{24,16},{28,20},{9,1},{13,5},{17,9},{2... | collective-permute-start | bytes 786440 | tf_op jit(solution)/shard_map/ppermute | solution.py:16
  21.5 0.6 copy-start.8
  72.2 22.0 %copy-start.12 = (s32[2,3]{1,0:T(2,128)S(1)}, s32[2,3]{1,0:T(2,128)}, u32[]{:S(2)}) copy-start(s32[2,3]{1,0:T(2,128)} %param.12) | copy-start | bytes 76
  92.6 20.3 %copy-start.6 = (s32[256]{0:T(256)S(1)}, s32[256]{0:T(256)}, u32[]{:S(2)}) copy-start(s32[256]{0:T(256)} %param.13) | copy-start | bytes 3076
  92.6 20.3 %copy-start.9 = (s32[256]{0:T(256)S(1)}, s32[256]{0:T(256)}, u32[]{:S(2)}) copy-start(s32[256]{0:T(256)} %copy-done.8) | copy-start | bytes 3076
  94.0 93.6 %reduce-scatter.2.cloned.1.call-start = ((), (), s32[]{:S(2)}) async-start(), calls=%async_computation.2 | async-start | bytes 1310720 | tf_op jit(solution)/shard_map/reduce_scatter | solution.py:120
  135.4 1.8 copy-start.1
  137.8 3.4 %copy-start.4 = (bf16[256,256]{0,1:T(8,128)(2,1)S(1)}, bf16[256,256]{0,1:T(8,128)(2,1)}, u32[]{:S(2)}) copy-start(bf16[256,256]{0,1:T(8,128)(2,1)} %copy.89) | copy-start | bytes 393220
  140.9 20.7 %copy-start.7 = (s32[256]{0:T(256)S(1)}, s32[256]{0:T(256)}, u32[]{:S(2)}) copy-start(s32[256]{0:T(256)} %param.13) | copy-start | bytes 3076
  140.9 20.7 %copy-start.10 = (s32[256]{0:T(256)S(1)}, s32[256]{0:T(256)}, u32[]{:S(2)}) copy-start(s32[256]{0:T(256)} %copy-done.8) | copy-start | bytes 3076
  140.9 20.7 %copy-start.11 = (pred[256]{0:T(512)(128)(4,1)S(1)}, pred[256]{0:T(512)(128)(4,1)}, u32[]{:S(2)}) copy-start(pred[256]{0:T(512)(128)(4,1)} %compare_reduce_fusion) | copy-start | bytes 772
Sparse Core Ops, SparseCore 0:
  94.1 66.4 all-reduce.3
  163.3 24.1 reduce-scatter.1
where the time goes:
time: 197 us; the launch traced here: 196 us
  blocking collectives  86.6 us (44%)
  waiting for transfers between devices  43.2 us (22%)
  local copies, waits for them, and re-layouts  21.8 us (11%)
  between operations  13.8 us (7%)
  starting transfers between devices  11.7 us (6%)
  matrix products  11.6 us (6%)
  other arithmetic  7.22 us (4%)
    psum x1, blocking collectives, shards(): lax.psum(jnp.dot(pick_table, projected, preferred_element_type=jnp.float3...  49.3 us
    reduce_scatter x1, waiting for transfers between devices, shards(): lax.psum_scatter(jnp.dot(attended, o_weight, preferred_element_type=jnp.f...  24.3 us
    pmax x1, blocking collectives, shards(): peak = lax.pmax(local_max, 'tm')  20.2 us
    psum x1, waiting for transfers between devices, shards(): lax.psum((local_totals * rescale, local_accum * rescale[..., None]), 'tm')  18.8 us
    psum x1, blocking collectives, shards(): lax.psum((local_totals * rescale, local_accum * rescale[..., None]), 'tm')  17.1 us
    ppermute x4, starting transfers between devices, shifted(): return lax.ppermute(block, axis, route)  11.6 us
    unnamed x34, local copies, waits for them, and re-layouts  7.5 us
    slice x2, local copies, waits for them, and re-layouts, shards(): gathered_keys[:, :, :feats]  4.04 us
  transfers between devices with their start and end apart: 6, of which 2 were waited for; matrix products, arithmetic and copies ran while one was open for 16% of the time, Pallas kernels for 0%

commit v1 on v0

v1 whole, which is shorter than its diff:
```python
import functools
import math

import jax
import jax.numpy as jnp
from jax import lax
from jax.experimental import pallas as pl
from jax.experimental.pallas import tpu as pltpu
from jax.sharding import PartitionSpec as P

HEAD_DIM = 64
BLOCK = 128
LANES = 128
NEVER = -1e30
RING_MOST = 16
VMEM_BYTES = 40 * 1024 * 1024


def project_kernel(t_ref, k_ref, v_ref, kv_ref, acc_ref):
    step = pl.program_id(0)
    feats = k_ref.shape[1]

    @pl.when(step == 0)
    def _():
        acc_ref[...] = jnp.zeros_like(acc_ref)

    rows = t_ref[...]
    acc_ref[:, :feats] += jnp.dot(rows, k_ref[...], preferred_element_type=jnp.float32)
    acc_ref[:, feats:] += jnp.dot(rows, v_ref[...], preferred_element_type=jnp.float32)

    @pl.when(step == pl.num_programs(0) - 1)
    def _():
        kv_ref[...] = acc_ref[...].astype(kv_ref.dtype)


def project(tokens, k_weight, v_weight):
    rows, depth = tokens.shape
    feats = k_weight.shape[1]
    part = depth // 4
    return pl.pallas_call(
        project_kernel,
        grid=(4,),
        out_shape=jax.ShapeDtypeStruct((rows, 2 * feats), jnp.bfloat16),
        in_specs=[
            pl.BlockSpec((rows, part), lambda i: (0, i)),
            pl.BlockSpec((part, feats), lambda i: (i, 0)),
            pl.BlockSpec((part, feats), lambda i: (i, 0)),
        ],
        out_specs=pl.BlockSpec((rows, 2 * feats), lambda i: (0, 0)),
        scratch_shapes=[pltpu.VMEM((rows, 2 * feats), jnp.float32)],
        compiler_params=pltpu.CompilerParams(vmem_limit_bytes=VMEM_BYTES),
    )(tokens, k_weight, v_weight)


def attend_kernel(slots, parts, here_ref, q_ref, bias_ref, glob_ref, *refs):
    kv_refs = refs[:slots]
    out_refs = refs[slots : slots + parts]
    table, peaks, sums, mixed = refs[slots + parts :]
    step = pl.program_id(0)
    rows, feats = q_ref.shape
    span = kv_refs[0].shape[0]
    per_shard = rows // BLOCK
    pairs = feats // LANES
    scale = HEAD_DIM ** (-0.5) * math.log2(math.e)

    @pl.when(step == 0)
    def _():
        peaks[...] = jnp.full_like(peaks, NEVER)
        sums[...] = jnp.zeros_like(sums)

    for j in range(per_shard):
        at = slice(j * BLOCK, (j + 1) * BLOCK)
        table[at, :] = jnp.where(glob_ref[at, :] > 0, 0.0, bias_ref[j : j + 1, :])

    lane = lax.broadcasted_iota(jnp.int32, (1, LANES), 1)

    def one_pair(pair, carry):
        lanes = pl.ds(pl.multiple_of(pair * LANES, LANES), LANES)
        v_lanes = pl.ds(pl.multiple_of(feats + pair * LANES, LANES), LANES)
        for odd in range(LANES // HEAD_DIM):
            head = pair * (LANES // HEAD_DIM) + odd
            mine = (lane // HEAD_DIM) == odd
            q = jnp.where(mine, q_ref[:, lanes], jnp.zeros((), q_ref.dtype))
            scores = []
            peak = peaks[head]
            for i in range(slots):
                s = lax.dot_general(
                    q,
                    kv_refs[i][:, lanes],
                    (((1,), (1,)), ((), ())),
                    preferred_element_type=jnp.float32,
                )
                s = s * scale + table[:, i * span : (i + 1) * span]
                scores.append(s)
            best = functools.reduce(jnp.maximum, [jnp.max(s, axis=1, keepdims=True) for s in scores])
            new = jnp.maximum(peak, best)
            total = sums[head] * jnp.exp2(peak - new)
            for i in range(slots):
                e = jnp.exp2(scores[i] - new[:, :1]).astype(jnp.bfloat16)
                v = jnp.where(mine, kv_refs[i][:, v_lanes], jnp.ones((), jnp.bfloat16))
                total = total + jnp.dot(e, v, preferred_element_type=jnp.float32)
            peaks[head] = new
            sums[head] = total
        return carry

    lax.fori_loop(0, pairs, one_pair, 0)

    @pl.when(step == pl.num_programs(0) - 1)
    def _():
        for pair in range(pairs):
            done = []
            for odd in range(LANES // HEAD_DIM):
                total = sums[pair * (LANES // HEAD_DIM) + odd]
                done.append(total / pltpu.roll(total, HEAD_DIM, 1))
            mixed[:, pair * LANES : (pair + 1) * LANES] = jnp.where(lane < HEAD_DIM, done[0], done[1])
        piece = rows // parts
        for d in range(parts):
            first = pl.multiple_of((here_ref[0] ^ d) * piece, piece)
            out_refs[d][...] = mixed[pl.ds(first, piece), :].astype(out_refs[d].dtype)


def attend(queries, bias, is_global, here, kvs, parts):
    rows, feats = queries.shape
    span = rows
    if isinstance(kvs, list):
        slots, steps = len(kvs), 1
        operands = kvs
    else:
        slots = 4
        steps = kvs.shape[0] // (slots * span)
        operands = [kvs] * slots

    def spot(i):
        return pl.BlockSpec((span, 2 * feats), lambda s: (s * slots + i if steps > 1 else 0, 0))

    heads = feats // HEAD_DIM
    return pl.pallas_call(
        functools.partial(attend_kernel, slots, parts),
        grid=(steps,),
        out_shape=[jax.ShapeDtypeStruct((rows // parts, feats), jnp.bfloat16)] * parts,
        in_specs=[
            pl.BlockSpec(memory_space=pltpu.SMEM),
            pl.BlockSpec((rows, feats), lambda s: (0, 0)),
            pl.BlockSpec((bias.shape[0], slots * span), lambda s: (0, s)),
            pl.BlockSpec((rows, 1), lambda s: (0, 0)),
        ]
        + [spot(i) for i in range(slots)],
        out_specs=[pl.BlockSpec((rows // parts, feats), lambda s: (0, 0))] * parts,
        scratch_shapes=[
            pltpu.VMEM((rows, slots * span), jnp.float32),
            pltpu.VMEM((heads, rows, LANES), jnp.float32),
            pltpu.VMEM((heads, rows, LANES), jnp.float32),
            pltpu.VMEM((rows, feats), jnp.float32),
        ],
        compiler_params=pltpu.CompilerParams(vmem_limit_bytes=VMEM_BYTES),
    )(here, queries, bias, is_global, *operands)


def mix_kernel(parts, *refs):
    total = None
    for i in range(parts):
        term = jnp.dot(refs[i][...], refs[parts + i][...], preferred_element_type=jnp.float32)
        total = term if total is None else total + term
    refs[2 * parts][...] = total.astype(refs[2 * parts].dtype)


def mix(pieces, o_blocks):
    parts = len(pieces)
    rows, columns = pieces[0].shape[0], o_blocks[0].shape[1]
    return pl.pallas_call(
        functools.partial(mix_kernel, parts),
        out_shape=jax.ShapeDtypeStruct((rows, columns), jnp.bfloat16),
        in_specs=[pl.BlockSpec(memory_space=pltpu.VMEM)] * (2 * parts),
        out_specs=pl.BlockSpec(memory_space=pltpu.VMEM),
        compiler_params=pltpu.CompilerParams(vmem_limit_bytes=VMEM_BYTES),
    )(*pieces, *o_blocks)


def swapped(block, axis, distance):
    return lax.ppermute(block, axis, [(i, i ^ distance) for i in range(lax.axis_size(axis))])


def turned(block, axis, distance):
    n = lax.axis_size(axis)
    return lax.ppermute(block, axis, [(i, (i + distance) % n) for i in range(n)])


def shards(tokens, q_weight, k_weight, v_weight, o_weight, rand_blocks, global_pos):
    tok_rows = tokens.shape[0]
    per_shard = tok_rows // BLOCK
    n = lax.axis_size("tm")
    me = lax.axis_index("tm")
    parts = lax.axis_size("head")
    here = lax.axis_index("head")

    kv = project(tokens, k_weight, v_weight)
    if n <= RING_MOST:
        column = [kv] + [turned(kv, "tm", 2 * k) for k in range(1, n // 2)]
        other = [swapped(block, "tm", 1) for block in column]
        kvs = column + other
        far = [(me - 2 * k) % n for k in range(n // 2)]
        held = jnp.stack(far + [shard ^ 1 for shard in far])
    else:
        kvs = lax.all_gather(kv, "tm", tiled=True)
        held = jnp.arange(n, dtype=jnp.int32)
    o_blocks = [o_weight] + [swapped(o_weight, "head", d) for d in range(1, parts)]

    queries = jnp.dot(tokens, q_weight, preferred_element_type=jnp.float32).astype(jnp.bfloat16)
    own = me * tok_rows + jnp.arange(tok_rows, dtype=jnp.int32)
    is_global = jnp.any(own[:, None] == global_pos[None, :], axis=1, keepdims=True)
    spots = (held[:, None] * tok_rows + jnp.arange(tok_rows, dtype=jnp.int32)[None, :]).reshape(-1)
    listed = jnp.any(spots[None, :] == global_pos[:, None], axis=0)
    key_block = spots // BLOCK
    block_ids = me * per_shard + jnp.arange(per_shard, dtype=jnp.int32)
    away = key_block[None, :] - block_ids[:, None]
    times = ((away >= -2) & (away <= 1)).astype(jnp.int32) + listed[None, :].astype(jnp.int32)
    for r in range(rand_blocks.shape[1]):
        times = times + (rand_blocks[:, r : r + 1] == key_block[None, :]).astype(jnp.int32)
    bias = jnp.where(times > 0, jnp.log2(jnp.maximum(times, 1).astype(jnp.float32)), NEVER)

    pieces = attend(
        queries, bias, is_global.astype(jnp.float32), here.reshape(1).astype(jnp.int32), kvs, parts
    )
    pieces = [pieces[0]] + [swapped(pieces[d], "head", d) for d in range(1, parts)]
    return mix(pieces, o_blocks)


def solution(mesh):
    placed = (
        P("tm", None),
        P(None, "head"),
        P(None, "head"),
        P(None, "head"),
        P("head", None),
        P("tm", None),
        P(),
    )
    return jax.shard_map(
        shards, mesh=mesh, in_specs=placed, out_specs=P(("tm", "head"), None), check_vma=False
    )
```

time: 197 us -> 63.6 us (0.32)
  blocking collectives: 86.6 us -> 0 us
  local copies, waits for them, and re-layouts: 21.8 us -> 4.98 us
  between operations: 13.8 us -> 0.15 us
  matrix products: 11.6 us -> 0.3 us
  waiting for transfers between devices: 43.2 us -> 34.9 us
  Pallas kernels: 0 us -> 8.03 us
  other arithmetic: 7.22 us -> 1.35 us
  starting transfers between devices: 11.7 us -> 13.7 us
    psum x2 -> x0, blocking collectives: 66.5 us -> none  [the longest x1 49.3 us: shards(): lax.psum(jnp.dot(pick_table, projected, preferred_element_type=jnp.float3...]
    ppermute x4 -> x13, waiting for transfers between devices: 0.01 us -> 34.9 us  [the longest x3 18.1 us: turned(): lax.ppermute(block, axis, [(i, (i + distance) % n) for i in range(n)])]
    reduce_scatter x1 -> x0, waiting for transfers between devices: 24.3 us -> none  [shards(): lax.psum_scatter(jnp.dot(attended, o_weight, preferred_element_type=jnp.f...]
    pmax x1 -> x0, blocking collectives: 20.2 us -> none  [shards(): peak = lax.pmax(local_max, 'tm')]
    psum x1 -> x0, waiting for transfers between devices: 18.8 us -> none  [shards(): lax.psum((local_totals * rescale, local_accum * rescale[..., None]), 'tm')]
    dot_general x10 -> x0, matrix products: 11.3 us -> none  [the longest x1 3.11 us: shards(): jnp.einsum('jhqk,jkhd->jqhd', near_exp.astype(jnp.bfloat16), near_v, pref...]
    pallas_call x0 -> x3, Pallas kernels: none -> 8.03 us  [the longest x1 5.76 us: attend(): pl.pallas_call(functools.partial(attend_kernel, slots, parts), grid=(step...]
    slice x7 -> x1, local copies, waits for them, and re-layouts: 5.61 us -> 0.18 us  [shards(): rand_blocks[:, r:r + 1] == key_block[None, :]]
  transfers between devices with their start and end apart: 6 -> 13, of which waited for: 2 -> 7; matrix products, arithmetic and copies ran while one was open for 16% -> 4% of each run, Pallas kernels for 0% -> 9%
where the time goes in v1:
time: 63.6 us; the launch traced here: 63.4 us
  waiting for transfers between devices  34.9 us (55%)
  starting transfers between devices  13.7 us (22%)
  Pallas kernels  8.03 us (13%)
  local copies, waits for them, and re-layouts  4.98 us (8%)
  other arithmetic  1.35 us (2%)
    ppermute x3, waiting for transfers between devices, turned(): lax.ppermute(block, axis, [(i, (i + distance) % n) for i in range(n)])  18.1 us
    ppermute x10, waiting for transfers between devices, swapped(): lax.ppermute(block, axis, [(i, i ^ distance) for i in range(lax.axis_size...  16.8 us
    ppermute x10, starting transfers between devices, swapped(): lax.ppermute(block, axis, [(i, i ^ distance) for i in range(lax.axis_size...  9.06 us
    pallas_call x1, Pallas kernels, attend(): pl.pallas_call(functools.partial(attend_kernel, slots, parts), grid=(step...  5.76 us
    ppermute x3, starting transfers between devices, turned(): lax.ppermute(block, axis, [(i, (i + distance) % n) for i in range(n)])  4.62 us
    unnamed x21, local copies, waits for them, and re-layouts  3.91 us
  transfers between devices with their start and end apart: 13, of which 7 were waited for; matrix products, arithmetic and copies ran while one was open for 4% of the time, Pallas kernels for 9%

profile of v1, /device:TPU:0, one launch (start us, length us, event | category | flops | bytes accessed | tf_op | source)
XLA Modules:
  0.0 63.4 jit_solution(1632167934023263237)
XLA Ops:
  0.0 1.1 %copy-done.1 = bf16[256,1024]{1,0:T(8,128)(2,1)S(1)} copy-done((bf16[256,1024]{1,0:T(8,128)(2,1)S(1)}, bf16[256,1024]{1,0:T(8,128)(2,1)}, u32[]{:S(2)}) %copy-start.1) | copy-done | bytes 524312
  1.1 1.0 %copy-done.3 = bf16[1024,256]{1,0:T(8,128)(2,1)S(1)} copy-done((bf16[1024,256]{1,0:T(8,128)(2,1)S(1)}, bf16[1024,256]{1,0:T(8,128)(2,1)}, u32[]{:S(2)}) %copy-start.3) | copy-done | bytes 524312
  2.1 1.0 %copy-done.4 = bf16[1024,256]{1,0:T(8,128)(2,1)S(1)} copy-done((bf16[1024,256]{1,0:T(8,128)(2,1)S(1)}, bf16[1024,256]{1,0:T(8,128)(2,1)}, u32[]{:S(2)}) %copy-start.4) | copy-done | bytes 524312
  3.2 1.1 %shard_map.73.refs_0_ = bf16[256,512]{1,0:T(8,128)(2,1)S(1)} custom-call(bf16[256,1024]{1,0:T(8,128)(2,1)S(1)} %copy-done.1, bf16[1024,256]{1,0:T(8,128)(2,1)S(1)} %copy-done.3, bf16[1024,256]{1,0:T(8,128)(2,1)S(1)} %copy-done.4), custom_call_target="tpu_custom_call" | custom-call | tf_op jit(solution)/shard_map/pallas_call | solution.py:40
  4.3 3.0 %collective-permute-start.3 = (bf16[256,512]{1,0:T(8,128)(2,1)S(1)}, bf16[256,512]{1,0:T(8,128)(2,1)S(1)}, u32[]{:S(2)}, u32[]{:S(2)}) collective-permute-start(bf16[256,512]{1,0:T(8,128)(2,1)S(1)} %shard_map.73.refs_0_), channel_id=1, source_target_pairs={{0,4},{4,0},{8,12},{12,8},{16,20},{20,16},{24,28},{28,24},{1,5},{5... | collective-permute-start | bytes 786440 | tf_op jit(solution)/shard_map/ppermute | solution.py:180
  7.4 3.6 %collective-permute-start.2 = (bf16[256,512]{1,0:T(8,128)(2,1)S(1)}, bf16[256,512]{1,0:T(8,128)(2,1)}, u32[]{:S(2)}, u32[]{:S(2)}) collective-permute-start(bf16[256,512]{1,0:T(8,128)(2,1)S(1)} %shard_map.73.refs_0_), channel_id=1, source_target_pairs={{0,24},{4,28},{8,0},{12,4},{16,8},{20,12},{24,16},{28,20},{1,25},{... | collective-permute-start | bytes 786440 | tf_op jit(solution)/shard_map/ppermute | solution.py:185
  11.0 1.0 %collective-permute-start = (bf16[256,512]{1,0:T(8,128)(2,1)S(1)}, bf16[256,512]{1,0:T(8,128)(2,1)}, u32[]{:S(2)}, u32[]{:S(2)}) collective-permute-start(bf16[256,512]{1,0:T(8,128)(2,1)S(1)} %shard_map.73.refs_0_), channel_id=1, source_target_pairs={{0,8},{4,12},{8,16},{12,20},{16,24},{20,28},{24,0},{28,4},{1,9},{5... | collective-permute-start | bytes 786440 | tf_op jit(solution)/shard_map/ppermute | solution.py:185
  12.0 1.5 %collective-permute-start.11 = (bf16[256,1024]{1,0:T(8,128)(2,1)S(1)}, bf16[256,1024]{1,0:T(8,128)(2,1)S(1)}, u32[]{:S(2)}, u32[]{:S(2)}) collective-permute-start(bf16[256,1024]{1,0:T(8,128)(2,1)S(1)} %copy-done.5), channel_id=1, source_target_pairs={{0,2},{1,3},{2,0},{3,1},{4,6},{5,7},{6,4},{7,5},{8,10},{9,11},{10,... | collective-permute-start | bytes 1572872 | tf_op jit(solution)/shard_map/ppermute | solution.py:180
  14.3 0.7 %copy-done.6 = bf16[256,512]{1,0:T(8,128)(2,1)} copy-done((bf16[256,512]{1,0:T(8,128)(2,1)}, bf16[256,512]{1,0:T(8,128)(2,1)S(1)}, u32[]{:S(2)}) %copy-start.6) | copy-done | bytes 262168
  15.0 2.8 %collective-permute-done.2.refs_3_ = bf16[256,512]{1,0:T(8,128)(2,1)} collective-permute-done((bf16[256,512]{1,0:T(8,128)(2,1)S(1)}, bf16[256,512]{1,0:T(8,128)(2,1)}, u32[]{:S(2)}, u32[]{:S(2)}) %collective-permute-start.2) | collective-permute-done | bytes 262176 | tf_op jit(solution)/shard_map/ppermute | solution.py:185
  17.8 15.3 %collective-permute-done.1.refs_2_ = bf16[256,512]{1,0:T(8,128)(2,1)} collective-permute-done((bf16[256,512]{1,0:T(8,128)(2,1)S(1)}, bf16[256,512]{1,0:T(8,128)(2,1)}, u32[]{:S(2)}, u32[]{:S(2)}) %collective-permute-start.1) | collective-permute-done | bytes 262176 | tf_op jit(solution)/shard_map/ppermute | solution.py:185
  33.1 0.5 collective-permute-start.6
  33.8 1.6 %collective-permute-start.5 = (bf16[256,512]{1,0:T(8,128)(2,1)}, bf16[256,512]{1,0:T(8,128)(2,1)}, u32[]{:S(2)}, u32[]{:S(2)}) collective-permute-start(bf16[256,512]{1,0:T(8,128)(2,1)} %collective-permute-done.1.refs_2_), channel_id=1, source_target_pairs={{0,4},{4,0},{8,12},{12,8},{16,20},{20,16},{24,28},{28,24},{1,5},{5... | collective-permute-start | bytes 786440 | tf_op jit(solution)/shard_map/ppermute | solution.py:180
  35.4 7.3 %collective-permute-done.6.refs_7_ = bf16[256,512]{1,0:T(8,128)(2,1)} collective-permute-done((bf16[256,512]{1,0:T(8,128)(2,1)}, bf16[256,512]{1,0:T(8,128)(2,1)}, u32[]{:S(2)}, u32[]{:S(2)}) %collective-permute-start.6) | collective-permute-done | bytes 262176 | tf_op jit(solution)/shard_map/ppermute | solution.py:180
  42.7 0.5 collective-permute-start.4
  43.4 0.6 convert_element_type.40
  43.9 0.8 %copy.9.glob_ref = f32[256,1]{1,0:T(8,128)S(1)} copy(f32[256,1]{0,1:T(1,128)} %bitcast.17) | data formatting | bytes 2048 | tf_op jit(solution)/shard_map/convert_element_type | solution.py:222
  45.1 3.2 %collective-permute-done.5.refs_6_ = bf16[256,512]{1,0:T(8,128)(2,1)} collective-permute-done((bf16[256,512]{1,0:T(8,128)(2,1)}, bf16[256,512]{1,0:T(8,128)(2,1)}, u32[]{:S(2)}, u32[]{:S(2)}) %collective-permute-start.5) | collective-permute-done | bytes 262176 | tf_op jit(solution)/shard_map/ppermute | solution.py:180
  48.3 3.2 %collective-permute-done.4.refs_5_ = bf16[256,512]{1,0:T(8,128)(2,1)} collective-permute-done((bf16[256,512]{1,0:T(8,128)(2,1)}, bf16[256,512]{1,0:T(8,128)(2,1)}, u32[]{:S(2)}, u32[]{:S(2)}) %collective-permute-start.4) | collective-permute-done | bytes 262176 | tf_op jit(solution)/shard_map/ppermute | solution.py:180
  51.5 5.8 %shard_map.74 = (bf16[64,256]{1,0:T(8,128)(2,1)S(1)}, bf16[64,256]{1,0:T(8,128)(2,1)S(1)}, bf16[64,256]{1,0:T(8,128)(2,1)S(1)}, bf16[64,256]{1,0:T(8,128)(2,1)S(1)}) custom-call(s32[1]{0:T(128)} %bitcast.here_ref, bf16[256,256]{1,0:T(8,128)(2,1)S(1)} %convolution_convert_fusion.q_ref, f32[2,2048]{1,0:T(2,128)S(1)} %compare_select_fusion.bias_ref, ...), custom_call_target="tpu_custom_call" | custom-call | tf_op jit(solution)/shard_map/pallas_call | solution.py:137
  57.4 1.6 %collective-permute-start.8 = (bf16[64,256]{1,0:T(8,128)(2,1)S(1)}, bf16[64,256]{1,0:T(8,128)(2,1)S(1)}, u32[]{:S(2)}, u32[]{:S(2)}) collective-permute-start(bf16[64,256]{1,0:T(8,128)(2,1)S(1)} %get-tuple-element.11), channel_id=1, source_target_pairs={{0,2},{1,3},{2,0},{3,1},{4,6},{5,7},{6,4},{7,5},{8,10},{9,11},{10,... | collective-permute-start | bytes 98312 | tf_op jit(solution)/shard_map/ppermute | solution.py:180
  59.2 2.1 %collective-permute-done.8.refs_2_ = bf16[64,256]{1,0:T(8,128)(2,1)S(1)} collective-permute-done((bf16[64,256]{1,0:T(8,128)(2,1)S(1)}, bf16[64,256]{1,0:T(8,128)(2,1)S(1)}, u32[]{:S(2)}, u32[]{:S(2)}) %collective-permute-start.8) | collective-permute-done | bytes 32800 | tf_op jit(solution)/shard_map/ppermute | solution.py:180
  61.3 0.9 %collective-permute-done.9.refs_3_ = bf16[64,256]{1,0:T(8,128)(2,1)S(1)} collective-permute-done((bf16[64,256]{1,0:T(8,128)(2,1)S(1)}, bf16[64,256]{1,0:T(8,128)(2,1)S(1)}, u32[]{:S(2)}, u32[]{:S(2)}) %collective-permute-start.9) | collective-permute-done | bytes 32800 | tf_op jit(solution)/shard_map/ppermute | solution.py:180
  62.3 1.1 %shard_map.75 = bf16[64,1024]{1,0:T(8,128)(2,1)} custom-call(bf16[64,256]{1,0:T(8,128)(2,1)S(1)} %get-tuple-element.9.refs_0_, bf16[64,256]{1,0:T(8,128)(2,1)S(1)} %collective-permute-done.7.refs_1_, bf16[64,256]{1,0:T(8,128)(2,1)S(1)} %collective-permute-done.8.refs_2_, bf16[64,256]{1,0:T(8,128)(2,1)S(1)} %collective-permute-done.9.refs_3_, ...), custom_call_target="tpu_custom_call" | custom-call | tf_op jit(solution)/shard_map/pallas_call | solution.py:170
  (40 shorter events, 1.8 us)
Async XLA Ops:
  0.0 44.7 %copy-start = (bf16[1024,256]{1,0:T(8,128)(2,1)S(1)}, bf16[1024,256]{1,0:T(8,128)(2,1)}, u32[]{:S(2)}) copy-start(bf16[1024,256]{1,0:T(8,128)(2,1)} %param.8) | copy-start | bytes 1572868
  0.0 1.1 %copy-start.1 = (bf16[256,1024]{1,0:T(8,128)(2,1)S(1)}, bf16[256,1024]{1,0:T(8,128)(2,1)}, u32[]{:S(2)}) copy-start(bf16[256,1024]{1,0:T(8,128)(2,1)} %t_ref.1) | copy-start | bytes 1572868
  1.1 1.0 %copy-start.3 = (bf16[1024,256]{1,0:T(8,128)(2,1)S(1)}, bf16[1024,256]{1,0:T(8,128)(2,1)}, u32[]{:S(2)}) copy-start(bf16[1024,256]{1,0:T(8,128)(2,1)} %k_ref.1) | copy-start | bytes 1572868
  2.1 1.0 %copy-start.4 = (bf16[1024,256]{1,0:T(8,128)(2,1)S(1)}, bf16[1024,256]{1,0:T(8,128)(2,1)}, u32[]{:S(2)}) copy-start(bf16[1024,256]{1,0:T(8,128)(2,1)} %v_ref.1) | copy-start | bytes 1572868
  3.2 8.8 %copy-start.5 = (bf16[256,1024]{1,0:T(8,128)(2,1)S(1)}, bf16[256,1024]{1,0:T(8,128)(2,1)}, u32[]{:S(2)}) copy-start(bf16[256,1024]{1,0:T(8,128)(2,1)} %refs_4_.1) | copy-start | bytes 1572868
  3.2 10.4 %copy-start.8 = (s32[2,3]{1,0:T(2,128)S(1)}, s32[2,3]{1,0:T(2,128)}, u32[]{:S(2)}) copy-start(s32[2,3]{1,0:T(2,128)} %param.12) | copy-start | bytes 76
  3.2 10.6 %copy-start.9 = (s32[256]{0:T(256)S(1)}, s32[256]{0:T(256)}, u32[]{:S(2)}) copy-start(s32[256]{0:T(256)} %param.13) | copy-start | bytes 3076
  3.2 41.6 %copy-start.2 = (bf16[256,1024]{1,0:T(8,128)(2,1)S(1)}, bf16[256,1024]{1,0:T(8,128)(2,1)}, u32[]{:S(2)}) copy-start(bf16[256,1024]{1,0:T(8,128)(2,1)} %t_ref.1) | copy-start | bytes 1572868
  4.3 9.9 %collective-permute-start.3 = (bf16[256,512]{1,0:T(8,128)(2,1)S(1)}, bf16[256,512]{1,0:T(8,128)(2,1)S(1)}, u32[]{:S(2)}, u32[]{:S(2)}) collective-permute-start(bf16[256,512]{1,0:T(8,128)(2,1)S(1)} %shard_map.73.refs_0_), channel_id=1, source_target_pairs={{0,4},{4,0},{8,12},{12,8},{16,20},{20,16},{24,28},{28,24},{1,5},{5... | collective-permute-start | bytes 786440 | tf_op jit(solution)/shard_map/ppermute | solution.py:180
  7.4 10.4 %collective-permute-start.2 = (bf16[256,512]{1,0:T(8,128)(2,1)S(1)}, bf16[256,512]{1,0:T(8,128)(2,1)}, u32[]{:S(2)}, u32[]{:S(2)}) collective-permute-start(bf16[256,512]{1,0:T(8,128)(2,1)S(1)} %shard_map.73.refs_0_), channel_id=1, source_target_pairs={{0,24},{4,28},{8,0},{12,4},{16,8},{20,12},{24,16},{28,20},{1,25},{... | collective-permute-start | bytes 786440 | tf_op jit(solution)/shard_map/ppermute | solution.py:185
  11.0 22.1 %collective-permute-start.1 = (bf16[256,512]{1,0:T(8,128)(2,1)S(1)}, bf16[256,512]{1,0:T(8,128)(2,1)}, u32[]{:S(2)}, u32[]{:S(2)}) collective-permute-start(bf16[256,512]{1,0:T(8,128)(2,1)S(1)} %shard_map.73.refs_0_), channel_id=1, source_target_pairs={{0,16},{4,20},{8,24},{12,28},{16,0},{20,4},{24,8},{28,12},{1,17},{... | collective-permute-start | bytes 786440 | tf_op jit(solution)/shard_map/ppermute | solution.py:185
  11.0 22.8 %collective-permute-start = (bf16[256,512]{1,0:T(8,128)(2,1)S(1)}, bf16[256,512]{1,0:T(8,128)(2,1)}, u32[]{:S(2)}, u32[]{:S(2)}) collective-permute-start(bf16[256,512]{1,0:T(8,128)(2,1)S(1)} %shard_map.73.refs_0_), channel_id=1, source_target_pairs={{0,8},{4,12},{8,16},{12,20},{16,24},{20,28},{24,0},{28,4},{1,9},{5... | collective-permute-start | bytes 786440 | tf_op jit(solution)/shard_map/ppermute | solution.py:185
  12.0 46.9 %collective-permute-start.11 = (bf16[256,1024]{1,0:T(8,128)(2,1)S(1)}, bf16[256,1024]{1,0:T(8,128)(2,1)S(1)}, u32[]{:S(2)}, u32[]{:S(2)}) collective-permute-start(bf16[256,1024]{1,0:T(8,128)(2,1)S(1)} %copy-done.5), channel_id=1, source_target_pairs={{0,2},{1,3},{2,0},{3,1},{4,6},{5,7},{6,4},{7,5},{8,10},{9,11},{10,... | collective-permute-start | bytes 1572872 | tf_op jit(solution)/shard_map/ppermute | solution.py:180
  14.3 0.7 %copy-start.6 = (bf16[256,512]{1,0:T(8,128)(2,1)}, bf16[256,512]{1,0:T(8,128)(2,1)S(1)}, u32[]{:S(2)}) copy-start(bf16[256,512]{1,0:T(8,128)(2,1)S(1)} %collective-permute-done.3.refs_4_) | copy-start | bytes 786436
  15.0 44.3 %collective-permute-start.10 = (bf16[256,1024]{1,0:T(8,128)(2,1)S(1)}, bf16[256,1024]{1,0:T(8,128)(2,1)S(1)}, u32[]{:S(2)}, u32[]{:S(2)}) collective-permute-start(bf16[256,1024]{1,0:T(8,128)(2,1)S(1)} %copy-done.5), channel_id=1, source_target_pairs={{0,1},{1,0},{2,3},{3,2},{4,5},{5,4},{6,7},{7,6},{8,9},{9,8},{10,11... | collective-permute-start | bytes 1572872 | tf_op jit(solution)/shard_map/ppermute | solution.py:180
  17.8 41.5 %collective-permute-start.12 = (bf16[256,1024]{1,0:T(8,128)(2,1)S(1)}, bf16[256,1024]{1,0:T(8,128)(2,1)S(1)}, u32[]{:S(2)}, u32[]{:S(2)}) collective-permute-start(bf16[256,1024]{1,0:T(8,128)(2,1)S(1)} %copy-done.5), channel_id=1, source_target_pairs={{0,3},{1,2},{2,1},{3,0},{4,7},{5,6},{6,5},{7,4},{8,11},{9,10},{10,... | collective-permute-start | bytes 1572872 | tf_op jit(solution)/shard_map/ppermute | solution.py:180
  33.1 9.6 %collective-permute-start.6 = (bf16[256,512]{1,0:T(8,128)(2,1)}, bf16[256,512]{1,0:T(8,128)(2,1)}, u32[]{:S(2)}, u32[]{:S(2)}) collective-permute-start(bf16[256,512]{1,0:T(8,128)(2,1)} %collective-permute-done.2.refs_3_), channel_id=1, source_target_pairs={{0,4},{4,0},{8,12},{12,8},{16,20},{20,16},{24,28},{28,24},{1,5},{5... | collective-permute-start | bytes 786440 | tf_op jit(solution)/shard_map/ppermute | solution.py:180
  33.8 14.5 %collective-permute-start.5 = (bf16[256,512]{1,0:T(8,128)(2,1)}, bf16[256,512]{1,0:T(8,128)(2,1)}, u32[]{:S(2)}, u32[]{:S(2)}) collective-permute-start(bf16[256,512]{1,0:T(8,128)(2,1)} %collective-permute-done.1.refs_2_), channel_id=1, source_target_pairs={{0,4},{4,0},{8,12},{12,8},{16,20},{20,16},{24,28},{28,24},{1,5},{5... | collective-permute-start | bytes 786440 | tf_op jit(solution)/shard_map/ppermute | solution.py:180
  42.7 8.8 %collective-permute-start.4 = (bf16[256,512]{1,0:T(8,128)(2,1)}, bf16[256,512]{1,0:T(8,128)(2,1)}, u32[]{:S(2)}, u32[]{:S(2)}) collective-permute-start(bf16[256,512]{1,0:T(8,128)(2,1)} %collective-permute-done.refs_1_), channel_id=1, source_target_pairs={{0,4},{4,0},{8,12},{12,8},{16,20},{20,16},{24,28},{28,24},{1,5},{5... | collective-permute-start | bytes 786440 | tf_op jit(solution)/shard_map/ppermute | solution.py:180
  44.8 6.8 %copy-start.7 = (bf16[256,512]{1,0:T(8,128)(2,1)S(1)}, bf16[256,512]{1,0:T(8,128)(2,1)}, u32[]{:S(2)}) copy-start(bf16[256,512]{1,0:T(8,128)(2,1)} %copy-done.6) | copy-start | bytes 786436
  57.3 2.0 %collective-permute-start.7 = (bf16[64,256]{1,0:T(8,128)(2,1)S(1)}, bf16[64,256]{1,0:T(8,128)(2,1)S(1)}, u32[]{:S(2)}, u32[]{:S(2)}) collective-permute-start(bf16[64,256]{1,0:T(8,128)(2,1)S(1)} %get-tuple-element.10), channel_id=1, source_target_pairs={{0,1},{1,0},{2,3},{3,2},{4,5},{5,4},{6,7},{7,6},{8,9},{9,8},{10,11... | collective-permute-start | bytes 98312 | tf_op jit(solution)/shard_map/ppermute | solution.py:180
  57.4 4.0 %collective-permute-start.8 = (bf16[64,256]{1,0:T(8,128)(2,1)S(1)}, bf16[64,256]{1,0:T(8,128)(2,1)S(1)}, u32[]{:S(2)}, u32[]{:S(2)}) collective-permute-start(bf16[64,256]{1,0:T(8,128)(2,1)S(1)} %get-tuple-element.11), channel_id=1, source_target_pairs={{0,2},{1,3},{2,0},{3,1},{4,6},{5,7},{6,4},{7,5},{8,10},{9,11},{10,... | collective-permute-start | bytes 98312 | tf_op jit(solution)/shard_map/ppermute | solution.py:180
  58.9 3.3 %collective-permute-start.9 = (bf16[64,256]{1,0:T(8,128)(2,1)S(1)}, bf16[64,256]{1,0:T(8,128)(2,1)S(1)}, u32[]{:S(2)}, u32[]{:S(2)}) collective-permute-start(bf16[64,256]{1,0:T(8,128)(2,1)S(1)} %get-tuple-element.12), channel_id=1, source_target_pairs={{0,3},{1,2},{2,1},{3,0},{4,7},{5,6},{6,5},{7,4},{8,11},{9,10},{10,... | collective-permute-start | bytes 98312 | tf_op jit(solution)/shard_map/ppermute | solution.py:180

commit v2 on v0

v2 whole, which is shorter than its diff:
```python
import functools
import math

import jax
import jax.numpy as jnp
from jax import lax
from jax.experimental import pallas as pl
from jax.experimental.pallas import tpu as pltpu
from jax.sharding import Mesh
from jax.sharding import PartitionSpec as P

HEAD_DIM = 64
BLOCK = 128
LANES = 128
DIGIT = 128
TILE_ROWS = 16
NEVER = -1e30
MIB = 1024 * 1024
VMEM = pl.BlockSpec(memory_space=pltpu.VMEM)
SMEM = pl.BlockSpec(memory_space=pltpu.SMEM)
ANY = pl.BlockSpec(memory_space=pl.ANY)


def low_half():
    return lax.broadcasted_iota(jnp.int32, (1, LANES), 1) < HEAD_DIM


def half_turn(block):
    return pltpu.roll(block, HEAD_DIM, 1)


def project_kernel(chunks, place_ref, rand_ref, t_hbm, q_hbm, k_hbm, v_hbm, own_ref, *refs):
    sent_refs, (t_ref, w_ref, all_ref, sems) = refs[:-4], refs[-4:]
    rows, depth = t_ref.shape
    feats = w_ref.shape[2]
    heads = feats // HEAD_DIM
    part = depth // chunks
    copies = []
    for c in range(chunks):
        at = slice(c * part, (c + 1) * part)
        group = [pltpu.make_async_copy(t_hbm.at[:, at], t_ref.at[:, at], sems.at[c, 0])]
        for i, w_hbm in enumerate((q_hbm, k_hbm, v_hbm)):
            group.append(pltpu.make_async_copy(w_hbm.at[at, :], w_ref.at[i, at, :], sems.at[c, 1 + i]))
        for copy in group:
            copy.start()
        copies.append(group)
    totals = [None] * 3
    for c in range(chunks):
        at = slice(c * part, (c + 1) * part)
        for copy in copies[c]:
            copy.wait()
        for i in range(3):
            term = jnp.dot(t_ref[:, at], w_ref[i, at, :], preferred_element_type=jnp.float32)
            totals[i] = term if c == 0 else totals[i] + term
    q, k, v = totals
    low = low_half()
    for pair in range(heads // 2):
        at = slice(pair * LANES, (pair + 1) * LANES)
        q2, k2, v2 = q[:, at], k[:, at], v[:, at]
        top, bottom = q2[: rows // 2], q2[rows // 2 :]
        kv = (jnp.where(low, k2, half_turn(v2)), jnp.where(low, half_turn(k2), v2))
        qs = (jnp.where(low, top, half_turn(bottom)), jnp.where(low, half_turn(top), bottom))
        for odd in range(2):
            all_ref[2 * pair + odd, :rows, :] = kv[odd].astype(jnp.bfloat16)
            all_ref[2 * pair + odd, rows : rows + rows // 2, :] = qs[odd].astype(jnp.bfloat16)
    near = place_ref[0]
    digit_rows = sent_refs[0].shape[0] - rows - rows // 2
    row = lax.broadcasted_iota(jnp.int32, (digit_rows, LANES), 0)
    digits = jnp.zeros((digit_rows, LANES), jnp.float32)
    picks = rand_ref.shape[1]
    for j in range(rand_ref.shape[0]):
        for r in range(picks):
            at = 2 * (j * picks + r)
            value = rand_ref[j, r]
            digits = jnp.where(row == at, (value // DIGIT).astype(jnp.float32), digits)
            digits = jnp.where(row == at + 1, (value % DIGIT).astype(jnp.float32), digits)
    own_ref[...] = all_ref[near, :rows, :]
    for d in range(heads):
        sent_refs[d][: rows + rows // 2, :] = all_ref[near ^ d]
        sent_refs[d][rows + rows // 2 :, :] = digits.astype(jnp.bfloat16)


def project(place, rand_blocks, tokens, q_weight, k_weight, v_weight):
    rows, depth = tokens.shape
    feats = k_weight.shape[1]
    heads = feats // HEAD_DIM
    chunks = 4
    message = rows + rows // 2
    digit_rows = -(-2 * rand_blocks.size // TILE_ROWS) * TILE_ROWS
    return pl.pallas_call(
        functools.partial(project_kernel, chunks),
        in_specs=[SMEM, SMEM, ANY, ANY, ANY, ANY],
        out_specs=[VMEM] * (1 + heads),
        out_shape=[jax.ShapeDtypeStruct((rows, LANES), jnp.bfloat16)]
        + [jax.ShapeDtypeStruct((message + digit_rows, LANES), jnp.bfloat16)] * heads,
        scratch_shapes=[
            pltpu.VMEM((rows, depth), jnp.bfloat16),
            pltpu.VMEM((3, depth, feats), jnp.bfloat16),
            pltpu.VMEM((heads, message, LANES), jnp.bfloat16),
            pltpu.SemaphoreType.DMA((chunks, 4)),
        ],
        compiler_params=pltpu.CompilerParams(vmem_limit_bytes=56 * MIB),
        cost_estimate=pl.CostEstimate(
            flops=6 * rows * depth * feats, bytes_accessed=2 * depth * (rows + 3 * feats), transcendentals=0
        ),
    )(place, rand_blocks, tokens, q_weight, k_weight, v_weight)


def pack_kernel(*refs):
    out_ref = refs[-1]
    rows = out_ref.shape[0] // (len(refs) - 1)
    for i, ref in enumerate(refs[:-1]):
        out_ref[i * rows : (i + 1) * rows, :] = ref[:rows, :]


def pack(rows, messages):
    return pl.pallas_call(
        pack_kernel,
        in_specs=[VMEM] * len(messages),
        out_specs=VMEM,
        out_shape=jax.ShapeDtypeStruct((rows * len(messages), LANES), jnp.bfloat16),
        compiler_params=pltpu.CompilerParams(vmem_limit_bytes=32 * MIB),
    )(*messages)


def attend_kernel(heads, picks, plan, steps, fresh, parts, place_ref, listed_ref, glob_ref, *refs):
    messages, refs = refs[:heads], refs[heads:]
    old, refs = ([], refs) if fresh else (refs[:2], refs[2:])
    count = 1 + max(entry[0] for entry in plan)
    kv_refs, refs = refs[:count], refs[count:]
    if parts:
        out_ref, peaks, sums, q_ref, bias_ref = refs
    else:
        peaks, sums, q_ref, bias_ref = refs
    span = glob_ref.shape[0] // heads
    per_shard = span // BLOCK
    near, far = place_ref[0], place_ref[1]
    step = pl.program_id(0) if steps > 1 else 0
    scale = HEAD_DIM ** (-0.5) * math.log2(math.e)
    low = low_half()

    def once(when, body):
        if steps > 1:
            pl.when(step == when)(body)
        else:
            body()

    def begin():
        if fresh:
            peaks[...] = jnp.full_like(peaks, NEVER)
            sums[...] = jnp.zeros_like(sums)
        else:
            peaks[...] = old[0][...]
            sums[...] = old[1][...]
        for d in range(heads):
            packed = messages[d][span : span + span // 2, :].astype(jnp.float32)
            top = jnp.where(low, packed, 0.0)
            bottom = jnp.where(low, half_turn(packed), 0.0)
            q_ref[d * span : d * span + span // 2, :] = top.astype(q_ref.dtype)
            q_ref[d * span + span // 2 : (d + 1) * span, :] = bottom.astype(q_ref.dtype)

    once(0, begin)

    for d in range(heads):
        rand = messages[d][span + span // 2 :, :].astype(jnp.float32)
        for j in range(per_shard):
            block = (far * heads + (near ^ d)) * per_shard + j
            chosen = []
            for r in range(picks):
                at = 2 * (j * picks + r)
                chosen.append(rand[at : at + 1, :] * DIGIT + rand[at + 1 : at + 2, :])
            for i, (_, _, group, slot) in enumerate(plan):
                there = far if group == "own" else (far ^ 1 if group == "other" else step)
                for b in range(per_shard):
                    key_block = (there * heads + (near ^ slot)) * per_shard + b
                    away = key_block - block
                    window = jnp.where((away >= -2) & (away <= 1), 1.0, 0.0)
                    times = listed_ref[pl.ds(key_block, 1), :] + window
                    for pick in chosen:
                        times = times + jnp.where(pick == key_block.astype(jnp.float32), 1.0, 0.0)
                    value = jnp.where(times > 0, jnp.log2(jnp.maximum(times, 1.0)), NEVER)
                    at = d * per_shard + j
                    lanes = slice(i * span + b * BLOCK, i * span + (b + 1) * BLOCK)
                    bias_ref[at : at + 1, lanes] = value

    def one_tile(tile, carry):
        rows = pl.ds(pl.multiple_of(tile * span, span), span)
        q = q_ref[rows, :]
        glob = glob_ref[rows, :] > 0
        scores = []
        for i, (ref, first, _, _) in enumerate(plan):
            s = lax.dot_general(
                q,
                kv_refs[ref][first : first + span, :],
                (((1,), (1,)), ((), ())),
                preferred_element_type=jnp.float32,
            )
            halves = []
            for j in range(per_shard):
                at = slice(j * BLOCK, (j + 1) * BLOCK)
                bias = bias_ref[pl.ds(tile * per_shard + j, 1), i * span : (i + 1) * span]
                halves.append(s[at, :] * scale + jnp.where(glob[at, :], 0.0, bias))
            scores.append(jnp.concatenate(halves, axis=0))
        best = functools.reduce(jnp.maximum, scores)
        peak = peaks[rows, :]
        new = jnp.maximum(peak, jnp.max(best, axis=1, keepdims=True))
        total = sums[rows, :] * jnp.exp2(peak - new)
        for i, (ref, first, _, _) in enumerate(plan):
            e = jnp.exp2(scores[i] - new[:, :1]).astype(jnp.bfloat16)
            v = jnp.where(low, jnp.ones((), jnp.bfloat16), kv_refs[ref][first : first + span, :])
            total = total + jnp.dot(e, v, preferred_element_type=jnp.float32)
        peaks[rows, :] = new
        sums[rows, :] = total
        return carry

    lax.fori_loop(0, heads, one_tile, 0)

    def finish():
        total = sums[...]
        sums[...] = total / half_turn(total)
        piece = span // parts
        for other in range(heads):
            for part in range(parts):
                first = pl.multiple_of((near ^ other) * span, span) + part * piece
                top = sums[pl.ds(first, piece // 2), :]
                bottom = sums[pl.ds(first + piece // 2, piece // 2), :]
                packed = jnp.where(low, half_turn(top), bottom)
                out_ref[other * parts + part] = packed.astype(out_ref.dtype)

    if parts:
        once(steps - 1, finish)


def attend(place, picks, listed, is_global, messages, old, kvs, plan, steps, parts):
    heads = len(messages)
    rows = is_global.shape[0]
    span = rows // heads
    state = [jax.ShapeDtypeStruct((rows, LANES), jnp.float32)] * 2
    scratch = [
        pltpu.VMEM((rows, LANES), jnp.bfloat16),
        pltpu.VMEM((rows // BLOCK, len(plan) * span), jnp.float32),
    ]
    if parts:
        out_shape = jax.ShapeDtypeStruct((heads * parts, span // parts // 2, LANES), jnp.bfloat16)
        scratch = [pltpu.VMEM(each.shape, each.dtype) for each in state] + scratch
    else:
        out_shape = state
    if steps > 1:
        kv_specs = [pl.BlockSpec((rows, LANES), lambda s: (s, 0))]
        placing = dict(grid=(steps,))
    else:
        kv_specs = [VMEM] * len(kvs)
        placing = {}
    area = rows * len(plan) * span * steps
    return pl.pallas_call(
        functools.partial(attend_kernel, heads, picks, plan, steps, not old, parts),
        out_shape=out_shape,
        in_specs=[SMEM, VMEM, VMEM] + [VMEM] * (heads + len(old)) + kv_specs,
        out_specs=VMEM if parts else [VMEM] * 2,
        scratch_shapes=scratch,
        compiler_params=pltpu.CompilerParams(vmem_limit_bytes=32 * MIB),
        cost_estimate=pl.CostEstimate(
            flops=4 * area * LANES, bytes_accessed=8 * rows * LANES, transcendentals=area
        ),
        **placing,
    )(place, listed, is_global, *messages, *old, *kvs)


def mix_kernel(near_count, order, here_ref, got_ref, *refs):
    parts = len(order)
    half = got_ref.shape[1]
    low = low_half()
    total = None
    for i, d in enumerate(order):
        source = here_ref[0] ^ d
        columns = []
        for near in range(0, near_count, 2):
            even = got_ref[near * parts + source].astype(jnp.float32)
            odd = got_ref[(near + 1) * parts + source].astype(jnp.float32)
            top = jnp.where(low, even, half_turn(odd))
            bottom = jnp.where(low, half_turn(even), odd)
            columns.append(jnp.concatenate([top, bottom], axis=0).astype(jnp.bfloat16))
        rows = jnp.concatenate(columns, axis=1)
        term = jnp.dot(rows, refs[i][...], preferred_element_type=jnp.float32)
        total = term if total is None else total + term
    refs[parts][...] = total.astype(refs[parts].dtype)


def mix(here, got, o_blocks, order):
    parts = len(o_blocks)
    return pl.pallas_call(
        functools.partial(mix_kernel, got.shape[0] // parts, order),
        out_shape=jax.ShapeDtypeStruct((2 * got.shape[1], o_blocks[0].shape[1]), jnp.bfloat16),
        in_specs=[SMEM] + [VMEM] * (1 + parts),
        out_specs=VMEM,
        compiler_params=pltpu.CompilerParams(vmem_limit_bytes=32 * MIB),
    )(here, got, *o_blocks)


def swapped(block, axis, distance):
    return lax.ppermute(block, axis, [(i, i ^ distance) for i in range(lax.axis_size(axis))])


def shards(tokens, q_weight, k_weight, v_weight, o_weight, rand_blocks, global_pos):
    tok_rows = tokens.shape[0]
    per_shard = tok_rows // BLOCK
    far_count, heads, parts = (lax.axis_size(axis) for axis in ("far", "near", "head"))
    far, near, here = (lax.axis_index(axis).astype(jnp.int32) for axis in ("far", "near", "head"))
    place = jnp.stack([near, far])

    o_blocks, order = [o_weight], [0]
    distance = parts // 2
    while distance:
        o_blocks = o_blocks + [swapped(block, "head", distance) for block in o_blocks]
        order = order + [d ^ distance for d in order]
        distance //= 2

    own_kv, *sent = project(place, rand_blocks, tokens, q_weight, k_weight, v_weight)
    messages = [sent[0]] + [swapped(sent[d], "near", d) for d in range(1, heads)]

    inner = jnp.arange(tok_rows, dtype=jnp.int32)
    spots = jnp.arange(far_count * heads * tok_rows, dtype=jnp.int32)
    listed = jnp.any(spots[None, :] == global_pos[:, None], axis=0)
    listed = listed.astype(jnp.float32).reshape(-1, BLOCK)
    group = far * heads + (near ^ jnp.arange(heads, dtype=jnp.int32))
    own = (group[:, None] * tok_rows + inner[None, :]).reshape(-1)
    is_global = jnp.any(own[:, None] == global_pos[None, :], axis=1, keepdims=True)
    is_global = is_global.astype(jnp.float32)

    everyone = functools.partial(attend, place, rand_blocks.shape[1], listed, is_global, messages)
    if far_count == 2:
        own_far = swapped(own_kv, "far", 1)
        rest_far = swapped(pack(tok_rows, messages[1:]), "far", 1)
        plan = [(d, 0, "own", d) for d in range(heads)] + [(heads, 0, "other", 0)]
        old = everyone([], messages + [own_far], plan, 1, 0)
        plan = [(0, (d - 1) * tok_rows, "other", d) for d in range(1, heads)]
        out = everyone(old, [rest_far], plan, 1, parts)
    else:
        kvs = lax.all_gather(pack(tok_rows, messages), "far", tiled=True)
        plan = [(0, d * tok_rows, "step", d) for d in range(heads)]
        out = everyone([], [kvs], plan, far_count, parts)
    got = lax.all_to_all(out, ("near", "head"), 0, 0, tiled=True)
    return mix(here.reshape(1), got, o_blocks, order)


def solution(mesh):
    count, parts = mesh.devices.shape
    tm = ("far", "near")
    placed = (
        P(tm, None),
        P(None, "head"),
        P(None, "head"),
        P(None, "head"),
        P("head", None),
        P(tm, None),
        P(),
    )

    def run(tokens, q_weight, *rest):
        heads = q_weight.shape[1] // HEAD_DIM // parts
        split = Mesh(mesh.devices.reshape(count // heads, heads, parts), (*tm, "head"))
        body = jax.shard_map(
            shards, mesh=split, in_specs=placed, out_specs=P((*tm, "head"), None), check_vma=False
        )
        return body(tokens, q_weight, *rest)

    return run
```

time: 197 us -> 44.2 us (0.22)
  blocking collectives: 86.6 us -> 0 us
  waiting for transfers between devices: 43.2 us -> 12.5 us
  local copies, waits for them, and re-layouts: 21.8 us -> 0.25 us
  Pallas kernels: 0 us -> 14.4 us
  between operations: 13.8 us -> 0.09 us
  matrix products: 11.6 us -> 0 us
  other arithmetic: 7.22 us -> 1.45 us
  starting transfers between devices: 11.7 us -> 15.3 us
    psum x2 -> x0, blocking collectives: 66.5 us -> none  [the longest x1 49.3 us: shards(): lax.psum(jnp.dot(pick_table, projected, preferred_element_type=jnp.float3...]
    reduce_scatter x1 -> x0, waiting for transfers between devices: 24.3 us -> none  [shards(): lax.psum_scatter(jnp.dot(attended, o_weight, preferred_element_type=jnp.f...]
    pmax x1 -> x0, blocking collectives: 20.2 us -> none  [shards(): peak = lax.pmax(local_max, 'tm')]
    psum x1 -> x0, waiting for transfers between devices: 18.8 us -> none  [shards(): lax.psum((local_totals * rescale, local_accum * rescale[..., None]), 'tm')]
    pallas_call x0 -> x5, Pallas kernels: none -> 14.4 us  [the longest x2 9.34 us: attend(): pl.pallas_call(functools.partial(attend_kernel, heads, picks, plan, steps...]
    dot_general x11 -> x0, matrix products: 11.6 us -> none  [the longest x1 3.11 us: shards(): jnp.einsum('jhqk,jkhd->jqhd', near_exp.astype(jnp.bfloat16), near_v, pref...]
    unnamed x34 -> x9, local copies, waits for them, and re-layouts: 7.5 us -> 0.02 us
    all_to_all x0 -> x1, waiting for transfers between devices: none -> 6.28 us  [shards(): got = lax.all_to_all(out, ('near', 'head'), 0, 0, tiled=True)]
  transfers between devices with their start and end apart: 6 -> 9, of which waited for: 2 -> 4; matrix products, arithmetic and copies ran while one was open for 16% -> 4% of each run, Pallas kernels for 0% -> 30%
where the time goes in v2:
time: 44.2 us; the launch traced here: 44 us
  starting transfers between devices  15.3 us (35%)
  Pallas kernels  14.4 us (33%)
  waiting for transfers between devices  12.5 us (28%)
  other arithmetic  1.45 us (3%)
    ppermute x8, starting transfers between devices, swapped(): lax.ppermute(block, axis, [(i, i ^ distance) for i in range(lax.axis_size...  11.8 us
    pallas_call x2, Pallas kernels, attend(): pl.pallas_call(functools.partial(attend_kernel, heads, picks, plan, steps...  9.34 us
    all_to_all x1, waiting for transfers between devices, shards(): got = lax.all_to_all(out, ('near', 'head'), 0, 0, tiled=True)  6.28 us
    ppermute x8, waiting for transfers between devices, swapped(): lax.ppermute(block, axis, [(i, i ^ distance) for i in range(lax.axis_size...  6.17 us
    pallas_call x1, Pallas kernels, project(): pl.pallas_call(functools.partial(project_kernel, chunks), in_specs=[SMEM,...  3.91 us
    all_to_all x1, starting transfers between devices, shards(): got = lax.all_to_all(out, ('near', 'head'), 0, 0, tiled=True)  3.51 us
    pallas_call x1, Pallas kernels, mix(): pl.pallas_call(functools.partial(mix_kernel, got.shape[0] // parts, order...  1.18 us
  transfers between devices with their start and end apart: 9, of which 4 were waited for; matrix products, arithmetic and copies ran while one was open for 4% of the time, Pallas kernels for 30%

profile of v2, /device:TPU:0, one launch (start us, length us, event | category | flops | bytes accessed | tf_op | source)
XLA Modules:
  0.0 44.0 jit_solution(13235840696235752442)
XLA Ops:
  0.0 2.9 %collective-permute-start.5 = (bf16[256,1024]{1,0:T(8,128)(2,1)}, bf16[256,1024]{1,0:T(8,128)(2,1)S(1)}, u32[]{:S(2)}, u32[]{:S(2)}) collective-permute-start(bf16[256,1024]{1,0:T(8,128)(2,1)} %refs_0_.1), channel_id=1, source_target_pairs={{0,2},{1,3},{2,0},{3,1},{4,6},{5,7},{6,4},{7,5},{8,10},{9,11},{10,... | collective-permute-start | bytes 1572872 | tf_op jit(solution)/shard_map/ppermute | solution.py:301
  2.9 0.0 collective-permute-start.6
  2.9 0.6 %pad_add_fusion.place_ref = s32[2]{0:T(128)} fusion(s32[1]{0:T(128)} %bitcast.2, s32[1]{0:T(128)} %bitcast.1), kind=kLoop, calls=%fused_computation.5 | loop fusion | flops 2 | bytes 16 | tf_op jit(solution)/shard_map/stack | solution.py:309
  3.5 3.9 %shard_map.73 = (bf16[256,128]{1,0:T(8,128)(2,1)}, bf16[400,128]{1,0:T(8,128)(2,1)}, bf16[400,128]{1,0:T(8,128)(2,1)}, bf16[400,128]{1,0:T(8,128)(2,1)}, bf16[400,128]{1,0:T(8,128)(2,1)}) custom-call(s32[2]{0:T(128)} %pad_add_fusion.place_ref, s32[2,3]{1,0:T(2,128)} %rand_ref.1, bf16[256,1024]{1,0:T(8,128)(2,1)} %t_hbm.1, bf16[1024,256]{1,0:T(8,128)(2,1)} %q_hbm.1, ...), custom_call_target="tpu_custom_call" | custom-call | flops 402653184 | bytes 2097152 | tf_op jit(solution)/shard_map/pallas_call | solution.py:90
  7.4 1.6 %collective-permute-start = (bf16[400,128]{1,0:T(8,128)(2,1)}, bf16[400,128]{1,0:T(8,128)(2,1)S(1)}, u32[]{:S(2)}, u32[]{:S(2)}) collective-permute-start(bf16[400,128]{1,0:T(8,128)(2,1)} %get-tuple-element.13), channel_id=1, source_target_pairs={{0,4},{4,0},{8,12},{12,8},{1,5},{5,1},{9,13},{13,9},{2,6},{6,2},{1... | collective-permute-start | bytes 307208 | tf_op jit(solution)/shard_map/ppermute | solution.py:301
  9.0 1.6 %collective-permute-start.1 = (bf16[400,128]{1,0:T(8,128)(2,1)}, bf16[400,128]{1,0:T(8,128)(2,1)S(1)}, u32[]{:S(2)}, u32[]{:S(2)}) collective-permute-start(bf16[400,128]{1,0:T(8,128)(2,1)} %get-tuple-element.14), channel_id=1, source_target_pairs={{0,8},{4,12},{8,0},{12,4},{1,9},{5,13},{9,1},{13,5},{2,10},{6,14},... | collective-permute-start | bytes 307208 | tf_op jit(solution)/shard_map/ppermute | solution.py:301
  10.6 0.4 collective-permute-start.2
  11.0 0.4 fusion
  11.4 1.6 %collective-permute-done.refs_1_.refs_5_.refs_0_ = bf16[400,128]{1,0:T(8,128)(2,1)S(1)} collective-permute-done((bf16[400,128]{1,0:T(8,128)(2,1)}, bf16[400,128]{1,0:T(8,128)(2,1)S(1)}, u32[]{:S(2)}, u32[]{:S(2)}) %collective-permute-start) | collective-permute-done | bytes 102432 | tf_op jit(solution)/shard_map/ppermute | solution.py:301
  13.0 2.6 %collective-permute-start.3 = (bf16[256,128]{1,0:T(8,128)(2,1)}, bf16[256,128]{1,0:T(8,128)(2,1)S(1)}, u32[]{:S(2)}, u32[]{:S(2)}) collective-permute-start(bf16[256,128]{1,0:T(8,128)(2,1)} %get-tuple-element.16), channel_id=1, source_target_pairs={{0,16},{16,0},{1,17},{17,1},{2,18},{18,2},{3,19},{19,3},{4,20},{20... | collective-permute-start | bytes 196616 | tf_op jit(solution)/shard_map/ppermute | solution.py:301
  15.6 0.8 %collective-permute-done.2.refs_3_.refs_7_.refs_2_ = bf16[400,128]{1,0:T(8,128)(2,1)S(1)} collective-permute-done((bf16[400,128]{1,0:T(8,128)(2,1)}, bf16[400,128]{1,0:T(8,128)(2,1)S(1)}, u32[]{:S(2)}, u32[]{:S(2)}) %collective-permute-start.2) | collective-permute-done | bytes 102432 | tf_op jit(solution)/shard_map/ppermute | solution.py:301
  16.5 2.7 %collective-permute-start.4 = (bf16[768,128]{1,0:T(8,128)(2,1)S(1)}, bf16[768,128]{1,0:T(8,128)(2,1)S(1)}, u32[]{:S(2)}, u32[]{:S(2)}) collective-permute-start(bf16[768,128]{1,0:T(8,128)(2,1)S(1)} %shard_map.75), channel_id=1, source_target_pairs={{0,16},{16,0},{1,17},{17,1},{2,18},{18,2},{3,19},{19,3},{4,20},{20... | collective-permute-start | bytes 589832 | tf_op jit(solution)/shard_map/ppermute | solution.py:301
  19.2 0.0 collective-permute-done.5.refs_1_
  19.2 0.0 collective-permute-start.7
  19.2 0.1 add_bitcast_fusion
  19.2 0.4 compare_reduce_fusion
  19.6 0.2 copy.11.glob_ref
  19.9 4.6 %shard_map.74 = (f32[1024,128]{1,0:T(8,128)S(1)}, f32[1024,128]{1,0:T(8,128)S(1)}) custom-call(s32[2]{0:T(128)S(1)} %copy-done.2, f32[16,128]{1,0:T(8,128)S(1)} %convert_bitcast_fusion.listed_ref, f32[1024,1]{1,0:T(8,128)S(1)} %copy.11.glob_ref, bf16[400,128]{1,0:T(8,128)(2,1)S(1)} %copy-done.1, ...), custom_call_target="tpu_custom_call" | custom-call | flops 671088640 | bytes 1048576 | tf_op jit(solution)/shard_map/pallas_call | solution.py:255
  24.5 3.7 %collective-permute-done.4.refs_6_ = bf16[768,128]{1,0:T(8,128)(2,1)S(1)} collective-permute-done((bf16[768,128]{1,0:T(8,128)(2,1)S(1)}, bf16[768,128]{1,0:T(8,128)(2,1)S(1)}, u32[]{:S(2)}, u32[]{:S(2)}) %collective-permute-start.4) | collective-permute-done | bytes 196640 | tf_op jit(solution)/shard_map/ppermute | solution.py:301
  28.3 4.7 %shard_map.76 = bf16[16,32,128]{2,1,0:T(8,128)(2,1)} custom-call(s32[2]{0:T(128)S(1)} %copy-done.2, f32[16,128]{1,0:T(8,128)S(1)} %convert_bitcast_fusion.listed_ref, f32[1024,1]{1,0:T(8,128)S(1)} %copy.11.glob_ref, bf16[400,128]{1,0:T(8,128)(2,1)S(1)} %copy-done.1, bf16[400,128]{1,0:T(8,128)(2,1)S(1)} %collective-permute-done.refs_1_.refs_5_.refs_0_, ...), custom_call_target="tpu_custom_call" | custom-call | flops 402653184 | bytes 1048576 | tf_op jit(solution)/shard_map/pallas_call | solution.py:255
  33.0 3.5 %all-to-all-start = ((bf16[16,32,128]{2,1,0:T(8,128)(2,1)}), bf16[16,32,128]{2,1,0:T(8,128)(2,1)S(1)}, u32[]{:S(2)}, u32[]{:S(2)}) async-start(bf16[16,32,128]{2,1,0:T(8,128)(2,1)} %shard_map.76), calls=%async_computation | async-start | bytes 262144 | tf_op jit(solution)/shard_map/all_to_all | solution.py:342
  36.5 6.3 %all-to-all-done.got_ref = bf16[16,32,128]{2,1,0:T(8,128)(2,1)S(1)} async-done(((bf16[16,32,128]{2,1,0:T(8,128)(2,1)}), bf16[16,32,128]{2,1,0:T(8,128)(2,1)S(1)}, u32[]{:S(2)}, u32[]{:S(2)}) %all-to-all-start) | async-done | bytes 131104 | tf_op jit(solution)/shard_map/all_to_all | solution.py:342
  42.8 0.0 collective-permute-done.7.refs_3_
  42.8 1.2 %shard_map.77 = bf16[64,1024]{1,0:T(8,128)(2,1)} custom-call(s32[1]{0:T(128)} %bitcast.here_ref, bf16[16,32,128]{2,1,0:T(8,128)(2,1)S(1)} %all-to-all-done.got_ref, bf16[256,1024]{1,0:T(8,128)(2,1)S(1)} %copy-done, bf16[256,1024]{1,0:T(8,128)(2,1)S(1)} %collective-permute-done.5.refs_1_, bf16[256,1024]{1,0:T(8,128)(2,1)S(1)} %collective-permute-done.6.refs_2_, ...), custom_call_target="tpu_custom_call" | custom-call | tf_op jit(solution)/shard_map/pallas_call | solution.py:291
  (16 shorter events, 0.1 us)
Async XLA Ops:
  0.0 19.2 %collective-permute-start.5 = (bf16[256,1024]{1,0:T(8,128)(2,1)}, bf16[256,1024]{1,0:T(8,128)(2,1)S(1)}, u32[]{:S(2)}, u32[]{:S(2)}) collective-permute-start(bf16[256,1024]{1,0:T(8,128)(2,1)} %refs_0_.1), channel_id=1, source_target_pairs={{0,2},{1,3},{2,0},{3,1},{4,6},{5,7},{6,4},{7,5},{8,10},{9,11},{10,... | collective-permute-start | bytes 1572872 | tf_op jit(solution)/shard_map/ppermute | solution.py:301
  2.9 33.6 %collective-permute-start.6 = (bf16[256,1024]{1,0:T(8,128)(2,1)}, bf16[256,1024]{1,0:T(8,128)(2,1)S(1)}, u32[]{:S(2)}, u32[]{:S(2)}) collective-permute-start(bf16[256,1024]{1,0:T(8,128)(2,1)} %refs_0_.1), channel_id=1, source_target_pairs={{0,1},{1,0},{2,3},{3,2},{4,5},{5,4},{6,7},{7,6},{8,9},{9,8},{10,11... | collective-permute-start | bytes 1572872 | tf_op jit(solution)/shard_map/ppermute | solution.py:301
  3.5 7.5 %copy-start.3 = (s32[256]{0:T(256)S(1)}, s32[256]{0:T(256)}, u32[]{:S(2)}) copy-start(s32[256]{0:T(256)} %param.13) | copy-start | bytes 3076
  7.4 5.6 %collective-permute-start = (bf16[400,128]{1,0:T(8,128)(2,1)}, bf16[400,128]{1,0:T(8,128)(2,1)S(1)}, u32[]{:S(2)}, u32[]{:S(2)}) collective-permute-start(bf16[400,128]{1,0:T(8,128)(2,1)} %get-tuple-element.13), channel_id=1, source_target_pairs={{0,4},{4,0},{8,12},{12,8},{1,5},{5,1},{9,13},{13,9},{2,6},{6,2},{1... | collective-permute-start | bytes 307208 | tf_op jit(solution)/shard_map/ppermute | solution.py:301
  9.0 6.6 %collective-permute-start.1 = (bf16[400,128]{1,0:T(8,128)(2,1)}, bf16[400,128]{1,0:T(8,128)(2,1)S(1)}, u32[]{:S(2)}, u32[]{:S(2)}) collective-permute-start(bf16[400,128]{1,0:T(8,128)(2,1)} %get-tuple-element.14), channel_id=1, source_target_pairs={{0,8},{4,12},{8,0},{12,4},{1,9},{5,13},{9,1},{13,5},{2,10},{6,14},... | collective-permute-start | bytes 307208 | tf_op jit(solution)/shard_map/ppermute | solution.py:301
  10.6 5.8 %collective-permute-start.2 = (bf16[400,128]{1,0:T(8,128)(2,1)}, bf16[400,128]{1,0:T(8,128)(2,1)S(1)}, u32[]{:S(2)}, u32[]{:S(2)}) collective-permute-start(bf16[400,128]{1,0:T(8,128)(2,1)} %get-tuple-element.15), channel_id=1, source_target_pairs={{0,12},{4,8},{8,4},{12,0},{1,13},{5,9},{9,5},{13,1},{2,14},{6,10},... | collective-permute-start | bytes 307208 | tf_op jit(solution)/shard_map/ppermute | solution.py:301
  13.0 6.9 %copy-start.1 = (bf16[400,128]{1,0:T(8,128)(2,1)S(1)}, bf16[400,128]{1,0:T(8,128)(2,1)}, u32[]{:S(2)}) copy-start(bf16[400,128]{1,0:T(8,128)(2,1)} %get-tuple-element.12.refs_0_.refs_4_) | copy-start | bytes 307204
  13.0 6.9 %copy-start.2 = (s32[2]{0:T(128)S(1)}, s32[2]{0:T(128)}, u32[]{:S(2)}) copy-start(s32[2]{0:T(128)} %pad_add_fusion.place_ref) | copy-start | bytes 28
  13.0 6.8 %collective-permute-start.3 = (bf16[256,128]{1,0:T(8,128)(2,1)}, bf16[256,128]{1,0:T(8,128)(2,1)S(1)}, u32[]{:S(2)}, u32[]{:S(2)}) collective-permute-start(bf16[256,128]{1,0:T(8,128)(2,1)} %get-tuple-element.16), channel_id=1, source_target_pairs={{0,16},{16,0},{1,17},{17,1},{2,18},{18,2},{3,19},{19,3},{4,20},{20... | collective-permute-start | bytes 196616 | tf_op jit(solution)/shard_map/ppermute | solution.py:301
  16.5 11.8 %collective-permute-start.4 = (bf16[768,128]{1,0:T(8,128)(2,1)S(1)}, bf16[768,128]{1,0:T(8,128)(2,1)S(1)}, u32[]{:S(2)}, u32[]{:S(2)}) collective-permute-start(bf16[768,128]{1,0:T(8,128)(2,1)S(1)} %shard_map.75), channel_id=1, source_target_pairs={{0,16},{16,0},{1,17},{17,1},{2,18},{18,2},{3,19},{19,3},{4,20},{20... | collective-permute-start | bytes 589832 | tf_op jit(solution)/shard_map/ppermute | solution.py:301
  19.2 23.6 %collective-permute-start.7 = (bf16[256,1024]{1,0:T(8,128)(2,1)S(1)}, bf16[256,1024]{1,0:T(8,128)(2,1)S(1)}, u32[]{:S(2)}, u32[]{:S(2)}) collective-permute-start(bf16[256,1024]{1,0:T(8,128)(2,1)S(1)} %collective-permute-done.5.refs_1_), channel_id=1, source_target_pairs={{0,1},{1,0},{2,3},{3,2},{4,5},{5,4},{6,7},{7,6},{8,9},{9,8},{10,11... | collective-permute-start | bytes 1572872 | tf_op jit(solution)/shard_map/ppermute | solution.py:301
  28.3 14.5 %copy-start = (bf16[256,1024]{1,0:T(8,128)(2,1)S(1)}, bf16[256,1024]{1,0:T(8,128)(2,1)}, u32[]{:S(2)}) copy-start(bf16[256,1024]{1,0:T(8,128)(2,1)} %refs_0_.1) | copy-start | bytes 1572868
  33.0 9.8 %all-to-all-start = ((bf16[16,32,128]{2,1,0:T(8,128)(2,1)}), bf16[16,32,128]{2,1,0:T(8,128)(2,1)S(1)}, u32[]{:S(2)}, u32[]{:S(2)}) async-start(bf16[16,32,128]{2,1,0:T(8,128)(2,1)} %shard_map.76), calls=%async_computation | async-start | bytes 262144 | tf_op jit(solution)/shard_map/all_to_all | solution.py:342
